TPU v7x, 256 devices: a whole 4x4x8 slice. The times are simulated.
256 devices in a mesh: ctx: 32 (over z_hi, y, core), tp: 8 (over z_lo, x).
Axes of the slice: x: 4, y: 4, z: 8 (z_hi: 4, z_lo: 2; z = z_hi * 2 + z_lo), core: 2. Of those that a mesh axis runs over, the one named last changes fastest.
Arguments:
- q_proj: bfloat16 [8192, 8192], P('ctx', 'tp'), may hold values from -6 to 6
- k_proj: bfloat16 [8192, 8192], P('ctx', 'tp'), may hold values from -6 to 6
- v_proj: bfloat16 [8192, 8192], P('ctx', 'tp'), may hold values from -6 to 6
- filters: float32 [8192, 512], P('ctx', 'tp'), may hold values from -0.0625 to 0.0625
- lengths: int32 [512], P('tp'), may hold values from 1 to 8192, as said below
- skip_gain: float32 [8192], P('tp'), may hold values from -4 to 4
- out_weight: bfloat16 [8192, 4096], P('tp'), may hold values from -0.0625 to 0.0625
Outputs:
- projected: bfloat16 [8192, 4096], P(('ctx', 'tp'))
Inputs may be any that keep to these rules, and one draw needn't show every extreme that they name: `lengths`: some group's filter has exactly 8192 taps and some group's exactly 1.
All inputs are finite; a program needn't handle non-finite values.
Results may differ from a plain program's by a relative error of at most 0.014.
Values may be sent and summed in bfloat16 or wider, within the bound.
A program may use at most 128 MiB of HBM per device.

v0:
```python
import functools

import jax
import jax.numpy as jnp
import numpy as np
from jax import lax
from jax.experimental import pallas as pl
from jax.experimental.pallas import tpu as pltpu
from jax.sharding import PartitionSpec as P

MESH = pl.DeviceIdType.MESH
BF = jnp.bfloat16
F32 = jnp.float32

CTX = 32
TOK = 256
CH = 1024
GRP = 64
C16 = 16
OUT = 4096
HALF = OUT // 2
R = 32
Q = 8
RC = R // 2
SEQ = CTX * TOK
WIDE = SEQ + 256

ORDER = (0, 2, 4, 6, 1, 3, 5, 7)
PLACE = tuple(ORDER.index(i) for i in range(8))


def lane_swap():
    swap = np.zeros((8, 8, 16, 8, 8, 16), np.float32)
    for a in range(8):
        for b in range(8):
            for c in range(16):
                swap[a, b, c, PLACE[b], a, c] = 1.0
    return swap.reshape(CH, CH)


def exact_dot(left, right):
    return jnp.dot(left, right, preferred_element_type=F32)


def kernel(
    k_hbm, v_hbm, q_hbm, f_hbm, w_hbm, s_hbm, lens, skip, out,
    kbuf, vbuf, qbuf, fbuf, wbuf, swap, gated, stage,
    fsend, frecv, xsend, xrecv, wide, toep, xpad, xv, yacc, ysend, yrecv, mixed,
    za, zb, ra, rb, sa, sb, r2a, r2b,
    load_sem, f_sem, x_sem, y_sem, rs_send, rs_recv,
):
    me = lax.axis_index("ctx")
    tp = lax.axis_index("tp")
    zl, x = tp // 4, lax.rem(tp, 4)
    other = {"tp": (1 - zl) * 4 + x}

    def along_x(step):
        return {"tp": zl * 4 + lax.rem(x + step, 4)}

    barrier = pltpu.get_barrier_semaphore()

    @pl.loop(1, CTX)
    def _(step):
        pl.semaphore_signal(
            barrier, inc=1, device_id={"ctx": lax.rem(me + step, CTX)}, device_id_type=MESH
        )

    for step in (1, 2, 3):
        pl.semaphore_signal(barrier, inc=1, device_id=along_x(step), device_id_type=MESH)
    pl.semaphore_signal(barrier, inc=1, device_id=other, device_id_type=MESH)

    def load(source, target, index):
        copy = pltpu.make_async_copy(source, target, load_sem.at[index])
        copy.start()
        return copy

    f_load = load(f_hbm, fbuf, 0)
    k_load = load(k_hbm, kbuf, 1)
    v_load = load(v_hbm, vbuf, 2)
    s_load = load(s_hbm, swap, 3)
    q_load = load(q_hbm, qbuf, 4)
    w_load = load(w_hbm, wbuf, 5)

    f_load.wait()
    lag = me * TOK + lax.broadcasted_iota(jnp.int32, (TOK, GRP), 0)
    taps = jnp.where(lag < lens[...], fbuf[...], 0.0).astype(BF)
    row = lax.broadcasted_iota(jnp.int32, (TOK, TOK), 0)
    col = lax.broadcasted_iota(jnp.int32, (TOK, TOK), 1)
    flip = jnp.where(row + col == TOK - 1, 1.0, 0.0).astype(BF)
    back = lax.dot_general(
        taps, flip, (((0,), (0,)), ((), ())), preferred_element_type=F32
    ).astype(BF)
    row = lax.broadcasted_iota(jnp.int32, (128, GRP), 0)
    col = lax.broadcasted_iota(jnp.int32, (128, GRP), 1)
    rows = None
    for half in range(2):
        pick = jnp.where(row == 2 * col + half, 1.0, 0.0).astype(BF)
        part = exact_dot(pick, back[:, half * 128 : half * 128 + 128])
        rows = part if rows is None else rows + part
    for e in range(CTX):
        fsend[e] = rows[4 * e : 4 * e + 4]
    frecv[me] = fsend[me]

    pl.semaphore_wait(barrier, CTX - 1 + 4)

    def send_all(source, target, sems):
        @pl.loop(1, CTX)
        def _(step):
            e = lax.rem(me + step, CTX)
            pltpu.make_async_remote_copy(
                source.at[e], target.at[me], sems.at[0], sems.at[1],
                device_id={"ctx": e}, device_id_type=MESH,
            ).start()

    def waiter(source, target, sems):
        return pltpu.make_async_remote_copy(
            source.at[pl.ds(0, CTX - 1)], target.at[pl.ds(0, CTX - 1)], sems.at[0], sems.at[1],
            device_id={"ctx": lax.rem(me + 1, CTX)}, device_id_type=MESH,
        )

    send_all(fsend, frecv, f_sem)

    k_load.wait()
    v_load.wait()
    for i in range(Q):
        part = (kbuf[i * R : i * R + R].astype(F32) * vbuf[i * R : i * R + R].astype(F32)).astype(BF)
        gated[i * R : i * R + R] = part
        for o in range(8):
            stage[o * R : o * R + R, i * 128 : i * 128 + 128] = part[:, o * 128 : o * 128 + 128]
    s_load.wait()
    for g in range(2):
        packed = exact_dot(stage[...], swap[:, g * 512 : g * 512 + 512]).astype(BF)
        for o in range(8):
            for i in range(4):
                xsend[g, o * 4 + i] = packed[o * R : o * R + R, i * 128 : i * 128 + 128]
        xrecv[g, me] = xsend[g, me]
        send_all(xsend.at[g], xrecv.at[g], x_sem.at[g])

    waiter(fsend, frecv, f_sem).wait_recv()
    for g in range(2):
        for n in range(2 * CTX):
            tap_row = frecv[CTX - 1 - n // 2, g * 2 + n % 2 : g * 2 + n % 2 + 1, :]
            wide[:, n * 128 : n * 128 + 128] = jnp.broadcast_to(tap_row, (8, 128))
        wide[:, SEQ:] = jnp.zeros((8, WIDE - SEQ), F32)
        wide[...] = pltpu.roll(wide[...], WIDE - 7, 1, stride=1, stride_axis=0)

        @pl.loop(0, 8)
        def _(a):
            whole = wide[...]
            high = pltpu.roll(whole, WIDE - 120 + 16 * a, 1)
            low = pltpu.roll(whole, WIDE - 112 + 16 * a, 1)
            both = jnp.concatenate([high, low], axis=0).astype(BF)
            at = pl.multiple_of(a * 16, 16)
            toep[g, pl.ds(at + 128, 16), :] = both[:, :SEQ]
            toep[g, pl.ds(at, 16), :] = both[:, 128 : SEQ + 128]

    xpad[:, :128] = jnp.zeros((TOK, 128), BF)
    for g in range(2):
        waiter(xsend.at[g], xrecv.at[g], x_sem.at[g]).wait_recv()
        for b in range(CTX):
            stage[(b // 8) * R : (b // 8) * R + R, (b % 8) * 128 : (b % 8) * 128 + 128] = xrecv[g, b]
        blocks = exact_dot(stage[:128, :], swap[...]).astype(BF)
        for o in range(4):
            for i in range(Q):
                xpad[i * R : i * R + R, 128 + o * 128 : 256 + o * 128] = blocks[
                    o * R : o * R + R, PLACE[i] * 128 : PLACE[i] * 128 + 128
                ]
        for n in range(8):
            moved = xpad[...]
            if n < 7:
                moved = pltpu.roll(moved, 16 * (7 - n), 1)
            xv[n * TOK : n * TOK + TOK, :] = moved[:, 128:]
        for d in range(4):
            width = 512 - 128 * d
            part = exact_dot(toep[g, :, (24 - 8 * d) * TOK : (32 - 8 * d) * TOK], xv[:, :width])
            if d == 0:
                yacc[g] = part
            else:
                yacc[g, :, 128 * d :] = yacc[g, :, 128 * d :] + part

    for ck in range(2):
        for g in range(2):
            for o in range(4):
                for i in range(Q):
                    at = i * R + ck * RC
                    stage[g * 64 + o * RC : g * 64 + o * RC + RC, i * 128 : i * 128 + 128] = yacc[
                        g, at : at + RC, o * 128 : o * 128 + 128
                    ].astype(BF)
        packed = exact_dot(stage[:128, :], swap[...]).astype(BF)
        for g in range(2):
            for b in range(CTX):
                at = g * 64 + (b // 8) * RC
                lane = PLACE[b % 8] * 128
                ysend[ck, b, g] = packed[at : at + RC, lane : lane + 128]
        yrecv[ck, me] = ysend[ck, me]
        send_all(ysend.at[ck], yrecv.at[ck], y_sem.at[ck])

    def rs_copy(source, target, index, device):
        return pltpu.make_async_remote_copy(
            source, target, rs_send.at[index], rs_recv.at[index], device_id=device, device_id_type=MESH
        )

    def first_a(ck, step):
        return rs_copy(za.at[ck, lax.rem(x + step, 4)], ra.at[ck, step - 1], ck * 8 + step - 1, along_x(step))

    def first_b(ck):
        return rs_copy(zb.at[ck, 1 - zl], rb.at[ck], ck * 8 + 3, other)

    def second_a(ck):
        return rs_copy(sa.at[ck, 1 - zl], r2a.at[ck], ck * 8 + 4, other)

    def second_b(ck, step):
        return rs_copy(
            sb.at[ck, lax.rem(x + step, 4)], r2b.at[ck, step - 1], ck * 8 + 4 + step, along_x(step)
        )

    q_load.wait()
    w_load.wait()
    for ck in range(2):
        waiter(ysend.at[ck], yrecv.at[ck], y_sem.at[ck]).wait_recv()
        for e in range(CTX):
            for g in range(2):
                o, i = e // 4, (e % 4) * 2 + g
                stage[o * RC : o * RC + RC, i * 128 : i * 128 + 128] = yrecv[ck, e, g]
        field = exact_dot(stage[:128, :], swap[...])
        for i in range(Q):
            at = i * R + ck * RC
            for o in range(8):
                lane = slice(o * 128, o * 128 + 128)
                conv = field[o * RC : o * RC + RC, PLACE[i] * 128 : PLACE[i] * 128 + 128]
                direct = skip[:, lane] * gated[at : at + RC, lane].astype(F32)
                mixed[i * RC : i * RC + RC, lane] = (
                    qbuf[at : at + RC, lane].astype(F32) * (conv + direct)
                ).astype(BF)

        @pl.loop(0, HALF // 512)
        def _(t):
            cols = pl.ds(pl.multiple_of(t * 512, 512), 512)
            cols_b = pl.ds(pl.multiple_of(t * 512 + HALF, 512), 512)
            part = exact_dot(mixed[...], wbuf[:, cols]).astype(BF)
            part_b = exact_dot(mixed[...], wbuf[:, cols_b]).astype(BF)
            for p in range(8):
                za[ck, p % 4, p // 4, :, cols] = part[p * RC : p * RC + RC]
                zb[ck, p // 4, p % 4, :, cols] = part_b[p * RC : p * RC + RC]

        for step in (1, 2, 3):
            first_a(ck, step).start()
        first_b(ck).start()

    for ck in range(2):
        first_b(ck).wait_recv()
        for i in range(4):
            sb[ck, i] = (zb[ck, zl, i].astype(F32) + rb[ck, i].astype(F32)).astype(BF)
        for step in (1, 2, 3):
            second_b(ck, step).start()
        for step in (1, 2, 3):
            first_a(ck, step).wait_recv()
        for i in range(2):
            total = za[ck, x, i].astype(F32)
            for step in range(3):
                total = total + ra[ck, step, i].astype(F32)
            sa[ck, i] = total.astype(BF)
        second_a(ck).start()

    for ck in range(2):
        rows = slice(ck * RC, ck * RC + RC)
        second_a(ck).wait_recv()
        out[rows, :HALF] = (sa[ck, zl].astype(F32) + r2a[ck].astype(F32)).astype(BF)
        for step in (1, 2, 3):
            second_b(ck, step).wait_recv()
        total = sb[ck, x].astype(F32)
        for step in range(3):
            total = total + r2b[ck, step].astype(F32)
        out[rows, HALF:] = total.astype(BF)

    waiter(fsend, frecv, f_sem).wait_send()
    for i in range(2):
        waiter(xsend.at[i], xrecv.at[i], x_sem.at[i]).wait_send()
        waiter(ysend.at[i], yrecv.at[i], y_sem.at[i]).wait_send()
        for step in (1, 2, 3):
            first_a(i, step).wait_send()
            second_b(i, step).wait_send()
        first_b(i).wait_send()
        second_a(i).wait_send()


def shards(q_proj, k_proj, v_proj, filters, lengths, skip_gain, out_weight):
    swap = jnp.asarray(lane_swap(), BF)
    vmem = pl.BlockSpec(memory_space=pltpu.VMEM)
    hbm = pl.BlockSpec(memory_space=pl.ANY)
    dma = pltpu.SemaphoreType.DMA
    scratch = [
        pltpu.VMEM((TOK, CH), BF),
        pltpu.VMEM((TOK, CH), BF),
        pltpu.VMEM((TOK, CH), BF),
        pltpu.VMEM((TOK, GRP), F32),
        pltpu.VMEM((CH, OUT), BF),
        pltpu.VMEM((CH, CH), BF),
        pltpu.VMEM((TOK, CH), BF),
        pltpu.VMEM((TOK, CH), BF),
        pltpu.VMEM((CTX, 4, 128), F32),
        pltpu.VMEM((CTX, 4, 128), F32),
        pltpu.VMEM((2, CTX, R, 128), BF),
        pltpu.VMEM((2, CTX, R, 128), BF),
        pltpu.VMEM((8, WIDE), F32),
        pltpu.VMEM((2, TOK, SEQ), BF),
        pltpu.VMEM((TOK, 640), BF),
        pltpu.VMEM((8 * TOK, 512), BF),
        pltpu.VMEM((2, TOK, 512), F32),
        pltpu.VMEM((2, CTX, 2, RC, 128), BF),
        pltpu.VMEM((2, CTX, 2, RC, 128), BF),
        pltpu.VMEM((128, CH), BF),
        pltpu.VMEM((2, 4, 2, RC, HALF), BF),
        pltpu.VMEM((2, 2, 4, RC, HALF), BF),
        pltpu.VMEM((2, 3, 2, RC, HALF), BF),
        pltpu.VMEM((2, 4, RC, HALF), BF),
        pltpu.VMEM((2, 2, RC, HALF), BF),
        pltpu.VMEM((2, 4, RC, HALF), BF),
        pltpu.VMEM((2, RC, HALF), BF),
        pltpu.VMEM((2, 3, RC, HALF), BF),
        dma((6,)),
        dma((2,)),
        dma((2, 2)),
        dma((2, 2)),
        dma((16,)),
        dma((16,)),
    ]
    return pl.pallas_call(
        kernel,
        out_shape=jax.ShapeDtypeStruct((R, OUT), BF),
        in_specs=[hbm] * 6 + [vmem] * 2,
        out_specs=vmem,
        scratch_shapes=scratch,
        compiler_params=pltpu.CompilerParams(
            collective_id=0, has_side_effects=True, vmem_limit_bytes=56 << 20
        ),
        name="hyena",
    )(
        k_proj, v_proj, q_proj, filters, out_weight, swap,
        lengths.reshape(1, GRP), skip_gain.reshape(1, CH),
    )


def solution(mesh):
    return jax.shard_map(
        shards,
        mesh=mesh,
        in_specs=(
            P("ctx", "tp"),
            P("ctx", "tp"),
            P("ctx", "tp"),
            P("ctx", "tp"),
            P("tp"),
            P("tp"),
            P("tp", None),
        ),
        out_specs=P(("ctx", "tp"), None),
        check_vma=False,
    )
```

profile of v0, /device:TPU:24, one launch (start us, length us, event | category | flops | bytes accessed | tf_op | source)
XLA Modules:
  0.0 68.3 jit_solution(10648297809114282197)
XLA Ops:
  0.0 1.6 %copy.9.f_hbm = f32[256,64]{1,0:T(8,128)} copy(f32[256,64]{0,1:T(8,128)} %param.11) | data formatting | bytes 131072 | tf_op args[3]
  1.6 65.0 %hyena.1 = bf16[32,4096]{1,0:T(8,128)(2,1)} custom-call(bf16[256,1024]{1,0:T(8,128)(2,1)} %k_hbm.1, bf16[256,1024]{1,0:T(8,128)(2,1)} %v_hbm.1, bf16[256,1024]{1,0:T(8,128)(2,1)} %q_hbm.1, f32[256,64]{1,0:T(8,128)} %copy.9.f_hbm, bf16[1024,4096]{1,0:T(8,128)(2,1)} %w_hbm.1, bf16[1024,1024]{1,0:T(8,128)(2,1)} %constant.2.clone.s_hbm, s32[1,64]{1,0:T(1,128)} %bitcast.3, ...), custom_call_target="tpu_custom_call" | custom-call | tf_op jit(solution)/shard_map/hyena/pallas_call | solution.py:328
  66.6 1.7 %copy.11 = bf16[32,4096]{1,0:T(8,128)(2,1)} copy(bf16[32,4096]{1,0:T(8,128)(2,1)} %hyena.1) | data formatting | bytes 524288
where the time goes:
time: 68.5 us; the launch traced here: 68.3 us
  Pallas kernels  65 us (95%)
  local copies, waits for them, and re-layouts  3.26 us (5%)
    pallas_call x1, Pallas kernels, shards(): pl.pallas_call(kernel, out_shape=jax.ShapeDtypeStruct((R, OUT), BF), in_s...  65 us
    unnamed x2, local copies, waits for them, and re-layouts  3.26 us

commit v1 on v0

v1 whole, which is shorter than its diff:
```python
import functools

import jax
import jax.numpy as jnp
import numpy as np
from jax import lax
from jax.experimental import pallas as pl
from jax.experimental.pallas import tpu as pltpu
from jax.sharding import PartitionSpec as P

MESH = pl.DeviceIdType.MESH
BF = jnp.bfloat16
F32 = jnp.float32

CTX = 32
TOK = 256
CH = 1024
GRP = 64
C16 = 16
OUT = 4096
R = 32
Q = 8
RC = R // 2
SEQ = CTX * TOK
WIDE = SEQ + 256

ORDER = (0, 2, 4, 6, 1, 3, 5, 7)
PLACE = tuple(ORDER.index(i) for i in range(8))


ROUTES = (
    (0, 1280, ("x0", "x1", "z")),
    (1280, 1536, ("x1", "z", "x0")),
    (2816, 1280, ("z", "x0", "x1")),
)


def bit(tp, way):
    x = tp % 4
    if way == "z":
        return tp // 4
    return x // 2 if way == "x1" else (x + 1) // 2 % 2


def lane_swap():
    swap = np.zeros((8, 8, 16, 8, 8, 16), np.float32)
    for a in range(8):
        for b in range(8):
            for c in range(16):
                swap[a, b, c, PLACE[b], a, c] = 1.0
    return swap.reshape(CH, CH)


def exact_dot(left, right):
    return jnp.dot(left, right, preferred_element_type=F32)


def kernel(
    k_hbm, v_hbm, q_hbm, f_hbm, w_hbm, s_hbm, l_hbm, d_hbm, out,
    kbuf, vbuf, qbuf, fbuf, wbuf, swap, lens, skip, gated, stage,
    fsend, frecv, xsend, xrecv, wide, toep, xpad, xv, yacc, y0send, y0recv, y1send, y1recv, q_own, direct, mixed, zacc,
    *rest,
):
    sums, (load_sem, f_sem, x_sem, y_sem, rs_send, rs_recv) = rest[:-6], rest[-6:]
    me = lax.axis_index("ctx")
    tp = lax.axis_index("tp")
    zl, x = tp // 4, lax.rem(tp, 4)
    mine = {"x0": lax.rem((x + 1) // 2, 2), "x1": x // 2, "z": zl}
    partner = {
        "x0": {"tp": zl * 4 + x + 1 - 2 * lax.rem(x, 2)},
        "x1": {"tp": zl * 4 + 3 - x},
        "z": {"tp": (1 - zl) * 4 + x},
    }

    def load(source, target, index):
        copy = pltpu.make_async_copy(source, target, load_sem.at[index])
        copy.start()
        return copy

    k_load = load(k_hbm, kbuf, 0)
    v_load = load(v_hbm, vbuf, 1)
    s_load = load(s_hbm, swap, 2)
    f_load = load(f_hbm, fbuf, 3)
    l_load = load(l_hbm, lens, 4)
    d_load = load(d_hbm, skip, 5)

    barrier = pltpu.get_barrier_semaphore()

    @pl.loop(1, CTX)
    def _(step):
        pl.semaphore_signal(
            barrier, inc=1, device_id={"ctx": lax.rem(me + step, CTX)}, device_id_type=MESH
        )

    for way in ("x0", "x1", "z"):
        pl.semaphore_signal(barrier, inc=1, device_id=partner[way], device_id_type=MESH)

    def send_all(source, target, sems):
        for far in (2, 1, 3, 0):

            @pl.loop(0 if far else 1, 8)
            def _(near):
                e = lax.rem(me // 8 + far, 4) * 8
                e += lax.rem(me // 2 + near // 2, 4) * 2 + lax.rem(me + near, 2)
                pltpu.make_async_remote_copy(
                    source.at[e], target.at[me], sems.at[0], sems.at[1],
                    device_id={"ctx": e}, device_id_type=MESH,
                ).start()

    def waiter(source, target, sems):
        return pltpu.make_async_remote_copy(
            source.at[pl.ds(0, CTX - 1)], target.at[pl.ds(0, CTX - 1)], sems.at[0], sems.at[1],
            device_id={"ctx": lax.rem(me + 1, CTX)}, device_id_type=MESH,
        )

    k_load.wait()
    v_load.wait()
    for i in range(Q):
        part = (kbuf[i * R : i * R + R].astype(F32) * vbuf[i * R : i * R + R].astype(F32)).astype(BF)
        gated[i * R : i * R + R] = part
        for o in range(8):
            stage[o * R : o * R + R, i * 128 : i * 128 + 128] = part[:, o * 128 : o * 128 + 128]
    f_load.wait()
    l_load.wait()
    row = lax.broadcasted_iota(jnp.int32, (GRP, GRP), 0)
    col = lax.broadcasted_iota(jnp.int32, (GRP, GRP), 1)
    limit = jnp.sum(jnp.where(row == col, lens[...].astype(F32), 0.0), axis=1, keepdims=True)
    lag = (me * TOK + lax.broadcasted_iota(jnp.int32, (GRP, TOK), 1)).astype(F32)
    taps = jnp.where(lag < limit, fbuf[...], 0.0).astype(BF)
    row = lax.broadcasted_iota(jnp.int32, (TOK, TOK), 0)
    col = lax.broadcasted_iota(jnp.int32, (TOK, TOK), 1)
    flip = jnp.where(row + col == TOK - 1, 1.0, 0.0).astype(BF)
    back = exact_dot(taps, flip).astype(BF)
    row = lax.broadcasted_iota(jnp.int32, (128, GRP), 0)
    col = lax.broadcasted_iota(jnp.int32, (128, GRP), 1)
    rows = None
    for half in range(2):
        pick = jnp.where(row == 2 * col + half, 1.0, 0.0).astype(BF)
        part = exact_dot(pick, back[:, half * 128 : half * 128 + 128])
        rows = part if rows is None else rows + part
    for e in range(CTX):
        fsend[e] = rows[4 * e : 4 * e + 4]
    frecv[me] = fsend[me]

    s_load.wait()

    def send_group(g):
        packed = exact_dot(stage[...], swap[:, g * 512 : g * 512 + 512]).astype(BF)
        for o in range(8):
            for i in range(4):
                xsend[g, o * 4 + i] = packed[o * R : o * R + R, i * 128 : i * 128 + 128]
        xrecv[g, me] = xsend[g, me]
        if g == 0:
            pl.semaphore_wait(barrier, CTX - 1 + 3)
            send_all(fsend, frecv, f_sem)
        send_all(xsend.at[g], xrecv.at[g], x_sem.at[g])

    send_group(0)

    send_group(1)
    q_load = load(q_hbm, qbuf, 6)
    w_loads = [load(w_hbm.at[:, g], wbuf.at[g], 7 + g) for g in range(2)]
    waiter(fsend, frecv, f_sem).wait_recv()
    for g in range(2):
        for n in range(2 * CTX):
            tap_row = frecv[CTX - 1 - n // 2, g * 2 + n % 2 : g * 2 + n % 2 + 1, :]
            wide[:, n * 128 : n * 128 + 128] = jnp.broadcast_to(tap_row, (8, 128))
        wide[:, SEQ:] = jnp.zeros((8, WIDE - SEQ), F32)
        wide[...] = pltpu.roll(wide[...], WIDE - 7, 1, stride=1, stride_axis=0)

        @pl.loop(0, 8)
        def _(a):
            whole = wide[...]
            high = pltpu.roll(whole, WIDE - 120 + 16 * a, 1)
            low = pltpu.roll(whole, WIDE - 112 + 16 * a, 1)
            both = jnp.concatenate([high, low], axis=0).astype(BF)
            at = pl.multiple_of(a * 16, 16)
            toep[g, pl.ds(at + 128, 16), :] = both[:, :SEQ]
            toep[g, pl.ds(at, 16), :] = both[:, 128 : SEQ + 128]

    xpad[:, :128] = jnp.zeros((TOK, 128), BF)
    for g in range(2):
        waiter(xsend.at[g], xrecv.at[g], x_sem.at[g]).wait_recv()
        for b in range(CTX):
            stage[(b // 8) * R : (b // 8) * R + R, (b % 8) * 128 : (b % 8) * 128 + 128] = xrecv[g, b]
        blocks = exact_dot(stage[:128, :], swap[...]).astype(BF)
        for o in range(4):
            for i in range(Q):
                xpad[i * R : i * R + R, 128 + o * 128 : 256 + o * 128] = blocks[
                    o * R : o * R + R, PLACE[i] * 128 : PLACE[i] * 128 + 128
                ]
        for n in range(8):
            moved = xpad[...]
            if n < 7:
                moved = pltpu.roll(moved, 16 * (7 - n), 1)
            xv[n * TOK : n * TOK + TOK, :] = moved[:, 128:]
        acc = exact_dot(toep[g, :, 24 * TOK :], xv[...])
        yacc[...] = acc
        for d in range(1, 4):
            width = 512 - 128 * d
            part = exact_dot(toep[g, :, (24 - 8 * d) * TOK : (32 - 8 * d) * TOK], xv[:, :width])
            yacc[:, 128 * d :] = yacc[:, 128 * d :] + part

        for o in range(4):
            for i in range(Q):
                for ck in range(2):
                    at = i * R + ck * RC
                    to = ck * 64 + o * RC
                    stage[to : to + RC, i * 128 : i * 128 + 128] = yacc[
                        at : at + RC, o * 128 : o * 128 + 128
                    ].astype(BF)
        packed = exact_dot(stage[:128, :], swap[...]).astype(BF)
        for ck in range(2):
            for b in range(CTX):
                at = ck * 64 + (b // 8) * RC
                lane = PLACE[b % 8] * 128
                if g == 0:
                    y0send[b, ck * RC : ck * RC + RC] = packed[at : at + RC, lane : lane + 128]
                else:
                    y1send[ck, b] = packed[at : at + RC, lane : lane + 128]
            if g == 1:
                y1recv[ck, me] = y1send[ck, me]
                send_all(y1send.at[ck], y1recv.at[ck], y_sem.at[1 + ck])
        if g == 0:
            y0recv[me] = y0send[me]
            send_all(y0send, y0recv, y_sem.at[0])

    def hop(ck, t, step):
        whole, got0, kept1, got1, kept2, got2 = sums[6 * t : 6 * t + 6]
        way = ROUTES[t][2][step]
        source = (whole, kept1, kept2)[step].at[ck, 1 - mine[way]]
        target = (got0, got1, got2)[step].at[ck]
        index = (ck * 3 + t) * 3 + step
        return pltpu.make_async_remote_copy(
            source, target, rs_send.at[index], rs_recv.at[index],
            device_id=partner[way], device_id_type=MESH,
        )

    def add_up(ck, t, step):
        whole, got0, kept1, got1, kept2, got2 = sums[6 * t : 6 * t + 6]
        first, width, ways = ROUTES[t]
        own = mine[ways[step]]
        hop(ck, t, step).wait_recv()
        if step == 0:
            for i in range(2):
                for j in range(2):
                    kept1[ck, i, j] = (whole[ck, own, i, j].astype(F32) + got0[ck, i, j].astype(F32)).astype(BF)
        elif step == 1:
            for i in range(2):
                kept2[ck, i] = (kept1[ck, own, i].astype(F32) + got1[ck, i].astype(F32)).astype(BF)
        else:
            total = kept2[ck, own].astype(F32) + got2[ck].astype(F32)
            out[ck * RC : ck * RC + RC, first : first + width] = total.astype(BF)

    q_load.wait()
    d_load.wait()
    row = lax.broadcasted_iota(jnp.int32, (256, 256), 0)
    col = lax.broadcasted_iota(jnp.int32, (256, 256), 1)
    split = jnp.where(
        col == lax.rem(row // 16, 2) * 128 + row // 32 * 16 + lax.rem(row, 16), 1.0, 0.0
    ).astype(BF)
    for k in range(4):
        lane = slice(k * 256, k * 256 + 256)
        q_part = exact_dot(qbuf[:, lane], split).astype(BF)
        gated_part = exact_dot(gated[:, lane], split)
        left = jnp.broadcast_to(skip[:, lane], (16, 256))
        skip_part = jnp.zeros((16, 256), F32)
        for _ in range(3):
            term = left.astype(BF)
            left = left - term.astype(F32)
            skip_part = skip_part + exact_dot(term, split)
        for g in range(2):
            half = slice(g * 128, g * 128 + 128)
            to = slice(k * 128, k * 128 + 128)
            for ck in range(2):
                for i in range(Q):
                    at = i * R + ck * RC
                    rows = slice(ck * 128 + i * RC, ck * 128 + i * RC + RC)
                    q_own[g, rows, to] = q_part[at : at + RC, half]
                    direct[g, rows, to] = skip_part[:, half] * gated_part[at : at + RC, half]

    def mix(field, g, ck, count):
        for i in range(Q):
            rows = slice(ck * 128 + i * RC, ck * 128 + i * RC + RC)
            for o in range(4):
                lane = slice(o * 128, o * 128 + 128)
                at = o * count + (ck * RC if count == R else 0)
                conv = field[at : at + RC, PLACE[i] * 128 : PLACE[i] * 128 + 128]
                mixed[g, rows, lane] = (
                    q_own[g, rows, lane].astype(F32) * (conv + direct[g, rows, lane])
                ).astype(BF)

    waiter(y0send, y0recv, y_sem.at[0]).wait_recv()
    for e in range(CTX):
        o, i = e // 8, e % 8
        stage[o * R : o * R + R, i * 128 : i * 128 + 128] = y0recv[e]
    field = exact_dot(stage[:128, :], swap[...])
    for ck in range(2):
        mix(field, 0, ck, R)
    w_loads[0].wait()
    w_loads[1].wait()

    @pl.loop(0, OUT // 512)
    def _(n):
        cols = pl.ds(pl.multiple_of(n * 512, 512), 512)
        zacc[:, cols] = exact_dot(mixed[0], wbuf[0, :, :, cols].reshape(512, 512))

    for ck in range(2):
        waiter(y1send.at[ck], y1recv.at[ck], y_sem.at[1 + ck]).wait_recv()
        for e in range(CTX):
            o, i = e // 8, e % 8
            stage[o * RC : o * RC + RC, i * 128 : i * 128 + 128] = y1recv[ck, e]
        field = exact_dot(stage[:64, :], swap[...])
        mix(field, 1, ck, RC)
        chunk = slice(ck * 128, ck * 128 + 128)
        for t, (first, width, ways) in enumerate(ROUTES):
            whole = sums[6 * t]

            @pl.loop(0, width // 256)
            def _(n):
                at = pl.multiple_of(n * 256, 256)
                cols = pl.ds(at + first, 256)
                part = exact_dot(mixed[1, chunk, :], wbuf[1, :, :, cols].reshape(512, 256))
                part = (part + zacc[chunk, cols]).astype(BF)
                for p in range(8):
                    to = [bit(p, way) for way in ways]
                    whole[ck, to[0], to[1], to[2], :, pl.ds(at, 256)] = part[p * RC : p * RC + RC]

            hop(ck, t, 0).start()

    for step in range(3):
        for ck in range(2):
            for t in range(3):
                add_up(ck, t, step)
                if step < 2:
                    hop(ck, t, step + 1).start()

    waiter(fsend, frecv, f_sem).wait_send()
    waiter(y0send, y0recv, y_sem.at[0]).wait_send()
    for i in range(2):
        waiter(xsend.at[i], xrecv.at[i], x_sem.at[i]).wait_send()
        waiter(y1send.at[i], y1recv.at[i], y_sem.at[1 + i]).wait_send()
        for t in range(3):
            for step in range(3):
                hop(i, t, step).wait_send()


def shards(q_proj, k_proj, v_proj, filters, lengths, skip_gain, out_weight):
    swap = jnp.asarray(lane_swap(), BF)
    vmem = pl.BlockSpec(memory_space=pltpu.VMEM)
    hbm = pl.BlockSpec(memory_space=pl.ANY)
    dma = pltpu.SemaphoreType.DMA
    sums = []
    for _, width, _ in ROUTES:
        for lead in ((2, 2, 2), (2, 2), (2, 2), (2,), (2,), ()):
            sums.append(pltpu.VMEM((2,) + lead + (RC, width), BF))
    scratch = [
        pltpu.VMEM((TOK, CH), BF),
        pltpu.VMEM((TOK, CH), BF),
        pltpu.VMEM((TOK, CH), BF),
        pltpu.VMEM((GRP, TOK), F32),
        pltpu.VMEM((2, CTX, C16, OUT), BF),
        pltpu.VMEM((CH, CH), BF),
        pltpu.VMEM((1, GRP), jnp.int32),
        pltpu.VMEM((1, CH), F32),
        pltpu.VMEM((TOK, CH), BF),
        pltpu.VMEM((TOK, CH), BF),
        pltpu.VMEM((CTX, 4, 128), F32),
        pltpu.VMEM((CTX, 4, 128), F32),
        pltpu.VMEM((2, CTX, R, 128), BF),
        pltpu.VMEM((2, CTX, R, 128), BF),
        pltpu.VMEM((8, WIDE), F32),
        pltpu.VMEM((2, TOK, SEQ), BF),
        pltpu.VMEM((TOK, 640), BF),
        pltpu.VMEM((8 * TOK, 512), BF),
        pltpu.VMEM((TOK, 512), F32),
        pltpu.VMEM((CTX, R, 128), BF),
        pltpu.VMEM((CTX, R, 128), BF),
        pltpu.VMEM((2, CTX, RC, 128), BF),
        pltpu.VMEM((2, CTX, RC, 128), BF),
        pltpu.VMEM((2, TOK, 512), BF),
        pltpu.VMEM((2, TOK, 512), F32),
        pltpu.VMEM((2, TOK, 512), BF),
        pltpu.VMEM((TOK, OUT), F32),
        *sums,
        dma((9,)),
        dma((2,)),
        dma((2, 2)),
        dma((3, 2)),
        dma((18,)),
        dma((18,)),
    ]
    return pl.pallas_call(
        kernel,
        out_shape=jax.ShapeDtypeStruct((R, OUT), BF),
        in_specs=[hbm] * 8,
        out_specs=vmem,
        scratch_shapes=scratch,
        compiler_params=pltpu.CompilerParams(
            collective_id=0, has_side_effects=True, vmem_limit_bytes=56 << 20
        ),
        name="hyena",
    )(
        k_proj, v_proj, q_proj, filters.T, out_weight.reshape(CTX, 2, C16, OUT), swap,
        lengths.reshape(1, GRP), skip_gain.reshape(1, CH),
    )


def solution(mesh):
    return jax.shard_map(
        shards,
        mesh=mesh,
        in_specs=(
            P("ctx", "tp"),
            P("ctx", "tp"),
            P("ctx", "tp"),
            P("ctx", "tp"),
            P("tp"),
            P("tp"),
            P("tp", None),
        ),
        out_specs=P(("ctx", "tp"), None),
        check_vma=False,
    )
```

time: 68.5 us -> 66 us (0.964)
  the two profiles are of different devices: /device:TPU:24 before, /device:TPU:2 now
where the time goes in v1:
time: 66 us; the launch traced here: 65.7 us
  Pallas kernels  64 us (97%)
  local copies, waits for them, and re-layouts  1.67 us (3%)
    pallas_call x1, Pallas kernels, shards(): pl.pallas_call(kernel, out_shape=jax.ShapeDtypeStruct((R, OUT), BF), in_s...  64 us
    unnamed x1, local copies, waits for them, and re-layouts  1.67 us

profile of v1, /device:TPU:2, one launch (start us, length us, event | category | flops | bytes accessed | tf_op | source)
XLA Modules:
  0.0 65.7 jit_solution(7051436438628294024)
XLA Ops:
  0.0 64.0 %hyena.1 = bf16[32,4096]{1,0:T(8,128)(2,1)} custom-call(bf16[256,1024]{1,0:T(8,128)(2,1)} %k_hbm.1, bf16[256,1024]{1,0:T(8,128)(2,1)} %v_hbm.1, bf16[256,1024]{1,0:T(8,128)(2,1)} %q_hbm.1, f32[64,256]{1,0:T(8,128)} %bitcast.5, bf16[32,2,16,4096]{3,2,1,0:T(8,128)(2,1)} %bitcast.4, bf16[1024,1024]{1,0:T(8,128)(2,1)} %constant.2.clone.s_hbm, s32[1,64]{1,0:T(1,128)} %bitcast.7, ...), custom_call_target="tpu_custom_call" | custom-call | tf_op jit(solution)/shard_map/hyena/pallas_call | solution.py:393
  64.1 1.7 %copy.10 = bf16[32,4096]{1,0:T(8,128)(2,1)} copy(bf16[32,4096]{1,0:T(8,128)(2,1)} %hyena.1) | data formatting | bytes 524288

commit v2 on v1

--- a/solution.py
+++ b/solution.py
@@ -29,10 +29,14 @@
 
 
 ROUTES = (
-    (0, 1280, ("x0", "x1", "z")),
-    (1280, 1536, ("x1", "z", "x0")),
-    (2816, 1280, ("z", "x0", "x1")),
+    (0, 768, ("x0", "x1", "z")),
+    (768, 768, ("x1", "z", "x0")),
+    (1536, 768, ("z", "x0", "x1")),
+    (2304, 512, ("x0", "x1", "z")),
+    (2816, 768, ("x1", "z", "x0")),
+    (3584, 512, ("z", "x0", "x1")),
 )
+NR = len(ROUTES)
 
 
 def bit(tp, way):
@@ -58,10 +62,10 @@
 def kernel(
     k_hbm, v_hbm, q_hbm, f_hbm, w_hbm, s_hbm, l_hbm, d_hbm, out,
     kbuf, vbuf, qbuf, fbuf, wbuf, swap, lens, skip, gated, stage,
-    fsend, frecv, xsend, xrecv, wide, toep, xpad, xv, yacc, y0send, y0recv, y1send, y1recv, q_own, direct, mixed, zacc,
+    fsend, frecv, xsend, xrecv, wide, turned, toep, xpad, xv, yacc, y0send, y0recv, y1send, y1recv, q_own, direct, field0, mixed, zacc,
     *rest,
 ):
-    sums, (load_sem, f_sem, x_sem, y_sem, rs_send, rs_recv) = rest[:-6], rest[-6:]
+    sums, (obuf, load_sem, f_sem, x_sem, y_sem, rs_send, rs_recv, out_sem) = rest[:-8], rest[-8:]
     me = lax.axis_index("ctx")
     tp = lax.axis_index("tp")
     zl, x = tp // 4, lax.rem(tp, 4)
@@ -164,19 +168,44 @@
     for g in range(2):
         for n in range(2 * CTX):
             tap_row = frecv[CTX - 1 - n // 2, g * 2 + n % 2 : g * 2 + n % 2 + 1, :]
-            wide[:, n * 128 : n * 128 + 128] = jnp.broadcast_to(tap_row, (8, 128))
-        wide[:, SEQ:] = jnp.zeros((8, WIDE - SEQ), F32)
-        wide[...] = pltpu.roll(wide[...], WIDE - 7, 1, stride=1, stride_axis=0)
+            wide[:, n * 128 : n * 128 + 128] = jnp.broadcast_to(tap_row, (16, 128))
+        wide[:, SEQ:] = jnp.zeros((16, WIDE - SEQ), F32)
+        turned[...] = pltpu.roll(wide[...], WIDE - 15, 1, stride=1, stride_axis=0).astype(BF)
 
         @pl.loop(0, 8)
         def _(a):
-            whole = wide[...]
-            high = pltpu.roll(whole, WIDE - 120 + 16 * a, 1)
-            low = pltpu.roll(whole, WIDE - 112 + 16 * a, 1)
-            both = jnp.concatenate([high, low], axis=0).astype(BF)
-            at = pl.multiple_of(a * 16, 16)
-            toep[g, pl.ds(at + 128, 16), :] = both[:, :SEQ]
+            both = pltpu.roll(turned[...], WIDE - 112 + 16 * a, 1)
+            at = pl.multiple_of(lax.rem(a, 2) * 128 + a // 2 * 16, 16)
+            toep[g, pl.ds(at + 64, 16), :] = both[:, :SEQ]
             toep[g, pl.ds(at, 16), :] = both[:, 128 : SEQ + 128]
+
+    def split_groups():
+        q_load.wait()
+        d_load.wait()
+        row = lax.broadcasted_iota(jnp.int32, (256, 256), 0)
+        col = lax.broadcasted_iota(jnp.int32, (256, 256), 1)
+        split = jnp.where(
+            col == lax.rem(row // 16, 2) * 128 + row // 32 * 16 + lax.rem(row, 16), 1.0, 0.0
+        ).astype(BF)
+        for k in range(4):
+            lane = slice(k * 256, k * 256 + 256)
+            q_part = exact_dot(qbuf[:, lane], split).astype(BF)
+            gated_part = exact_dot(gated[:, lane], split)
+            left = jnp.broadcast_to(skip[:, lane], (16, 256))
+            skip_part = jnp.zeros((16, 256), F32)
+            for _ in range(3):
+                term = left.astype(BF)
+                left = left - term.astype(F32)
+                skip_part = skip_part + exact_dot(term, split)
+            for g in range(2):
+                half = slice(g * 128, g * 128 + 128)
+                to = slice(k * 128, k * 128 + 128)
+                for ck in range(2):
+                    for i in range(Q):
+                        at = i * R + ck * RC
+                        rows = slice(ck * 128 + i * RC, ck * 128 + i * RC + RC)
+                        q_own[g, rows, to] = q_part[at : at + RC, half]
+                        direct[g, rows, to] = skip_part[:, half] * gated_part[at : at + RC, half]
 
     xpad[:, :128] = jnp.zeros((TOK, 128), BF)
     for g in range(2):
@@ -194,46 +223,64 @@
             if n < 7:
                 moved = pltpu.roll(moved, 16 * (7 - n), 1)
             xv[n * TOK : n * TOK + TOK, :] = moved[:, 128:]
-        acc = exact_dot(toep[g, :, 24 * TOK :], xv[...])
-        yacc[...] = acc
-        for d in range(1, 4):
-            width = 512 - 128 * d
-            part = exact_dot(toep[g, :, (24 - 8 * d) * TOK : (32 - 8 * d) * TOK], xv[:, :width])
-            yacc[:, 128 * d :] = yacc[:, 128 * d :] + part
-
-        for o in range(4):
-            for i in range(Q):
-                for ck in range(2):
-                    at = i * R + ck * RC
-                    to = ck * 64 + o * RC
+        def convolve(rows):
+            yacc[rows] = exact_dot(toep[g, rows, 24 * TOK :], xv[...])
+            for d in range(1, 4):
+                width = 512 - 128 * d
+                part = exact_dot(toep[g, rows, (24 - 8 * d) * TOK : (32 - 8 * d) * TOK], xv[:, :width])
+                yacc[rows, 128 * d :] = yacc[rows, 128 * d :] + part
+
+        def pack(ck, start):
+            for o in range(4):
+                for i in range(Q):
+                    at = ck * 128 + i * RC
+                    to = start + o * RC
                     stage[to : to + RC, i * 128 : i * 128 + 128] = yacc[
                         at : at + RC, o * 128 : o * 128 + 128
                     ].astype(BF)
-        packed = exact_dot(stage[:128, :], swap[...]).astype(BF)
-        for ck in range(2):
-            for b in range(CTX):
-                at = ck * 64 + (b // 8) * RC
-                lane = PLACE[b % 8] * 128
-                if g == 0:
+
+        if g == 0:
+            convolve(slice(0, TOK))
+            pack(0, 0)
+            pack(1, 64)
+            packed = exact_dot(stage[:128, :], swap[...]).astype(BF)
+            for ck in range(2):
+                for b in range(CTX):
+                    at = ck * 64 + (b // 8) * RC
+                    lane = PLACE[b % 8] * 128
                     y0send[b, ck * RC : ck * RC + RC] = packed[at : at + RC, lane : lane + 128]
-                else:
+            y0recv[me] = y0send[me]
+            send_all(y0send, y0recv, y_sem.at[0])
+            split_groups()
+        else:
+            for ck in range(2):
+                convolve(slice(ck * 128, ck * 128 + 128))
+                pack(ck, 0)
+                packed = exact_dot(stage[:64, :], swap[...]).astype(BF)
+                for b in range(CTX):
+                    at = (b // 8) * RC
+                    lane = PLACE[b % 8] * 128
                     y1send[ck, b] = packed[at : at + RC, lane : lane + 128]
-            if g == 1:
                 y1recv[ck, me] = y1send[ck, me]
                 send_all(y1send.at[ck], y1recv.at[ck], y_sem.at[1 + ck])
-        if g == 0:
-            y0recv[me] = y0send[me]
-            send_all(y0send, y0recv, y_sem.at[0])
 
     def hop(ck, t, step):
         whole, got0, kept1, got1, kept2, got2 = sums[6 * t : 6 * t + 6]
         way = ROUTES[t][2][step]
         source = (whole, kept1, kept2)[step].at[ck, 1 - mine[way]]
         target = (got0, got1, got2)[step].at[ck]
-        index = (ck * 3 + t) * 3 + step
+        index = (ck * NR + t) * 3 + step
         return pltpu.make_async_remote_copy(
             source, target, rs_send.at[index], rs_recv.at[index],
             device_id=partner[way], device_id_type=MESH,
+        )
+
+    def store(ck, t):
+        first, width, _ = ROUTES[t]
+        return pltpu.make_async_copy(
+            obuf.at[ck, :, pl.ds(first, width)],
+            out.at[pl.ds(ck * RC, RC), pl.ds(first, width)],
+            out_sem.at[ck * NR + t],
         )
 
     def add_up(ck, t, step):
@@ -250,34 +297,8 @@
                 kept2[ck, i] = (kept1[ck, own, i].astype(F32) + got1[ck, i].astype(F32)).astype(BF)
         else:
             total = kept2[ck, own].astype(F32) + got2[ck].astype(F32)
-            out[ck * RC : ck * RC + RC, first : first + width] = total.astype(BF)
-
-    q_load.wait()
-    d_load.wait()
-    row = lax.broadcasted_iota(jnp.int32, (256, 256), 0)
-    col = lax.broadcasted_iota(jnp.int32, (256, 256), 1)
-    split = jnp.where(
-        col == lax.rem(row // 16, 2) * 128 + row // 32 * 16 + lax.rem(row, 16), 1.0, 0.0
-    ).astype(BF)
-    for k in range(4):
-        lane = slice(k * 256, k * 256 + 256)
-        q_part = exact_dot(qbuf[:, lane], split).astype(BF)
-        gated_part = exact_dot(gated[:, lane], split)
-        left = jnp.broadcast_to(skip[:, lane], (16, 256))
-        skip_part = jnp.zeros((16, 256), F32)
-        for _ in range(3):
-            term = left.astype(BF)
-            left = left - term.astype(F32)
-            skip_part = skip_part + exact_dot(term, split)
-        for g in range(2):
-            half = slice(g * 128, g * 128 + 128)
-            to = slice(k * 128, k * 128 + 128)
-            for ck in range(2):
-                for i in range(Q):
-                    at = i * R + ck * RC
-                    rows = slice(ck * 128 + i * RC, ck * 128 + i * RC + RC)
-                    q_own[g, rows, to] = q_part[at : at + RC, half]
-                    direct[g, rows, to] = skip_part[:, half] * gated_part[at : at + RC, half]
+            obuf[ck, :, first : first + width] = total.astype(BF)
+            store(ck, t).start()
 
     def mix(field, g, ck, count):
         for i in range(Q):
@@ -294,18 +315,21 @@
     for e in range(CTX):
         o, i = e // 8, e % 8
         stage[o * R : o * R + R, i * 128 : i * 128 + 128] = y0recv[e]
-    field = exact_dot(stage[:128, :], swap[...])
-    for ck in range(2):
-        mix(field, 0, ck, R)
+    field0[...] = exact_dot(stage[:128, :], swap[...])
     w_loads[0].wait()
     w_loads[1].wait()
 
-    @pl.loop(0, OUT // 512)
-    def _(n):
-        cols = pl.ds(pl.multiple_of(n * 512, 512), 512)
-        zacc[:, cols] = exact_dot(mixed[0], wbuf[0, :, :, cols].reshape(512, 512))
+    def project_first(ck):
+        mix(field0, 0, ck, R)
+        chunk = slice(ck * 128, ck * 128 + 128)
+
+        @pl.loop(0, OUT // 512)
+        def _(n):
+            cols = pl.ds(pl.multiple_of(n * 512, 512), 512)
+            zacc[chunk, cols] = exact_dot(mixed[0, chunk, :], wbuf[0, :, :, cols].reshape(512, 512))
 
     for ck in range(2):
+        project_first(ck)
         waiter(y1send.at[ck], y1recv.at[ck], y_sem.at[1 + ck]).wait_recv()
         for e in range(CTX):
             o, i = e // 8, e % 8
@@ -330,7 +354,7 @@
 
     for step in range(3):
         for ck in range(2):
-            for t in range(3):
+            for t in range(NR):
                 add_up(ck, t, step)
                 if step < 2:
                     hop(ck, t, step + 1).start()
@@ -340,14 +364,14 @@
     for i in range(2):
         waiter(xsend.at[i], xrecv.at[i], x_sem.at[i]).wait_send()
         waiter(y1send.at[i], y1recv.at[i], y_sem.at[1 + i]).wait_send()
-        for t in range(3):
+        for t in range(NR):
             for step in range(3):
                 hop(i, t, step).wait_send()
+            store(i, t).wait()
 
 
 def shards(q_proj, k_proj, v_proj, filters, lengths, skip_gain, out_weight):
     swap = jnp.asarray(lane_swap(), BF)
-    vmem = pl.BlockSpec(memory_space=pltpu.VMEM)
     hbm = pl.BlockSpec(memory_space=pl.ANY)
     dma = pltpu.SemaphoreType.DMA
     sums = []
@@ -369,7 +393,8 @@
         pltpu.VMEM((CTX, 4, 128), F32),
         pltpu.VMEM((2, CTX, R, 128), BF),
         pltpu.VMEM((2, CTX, R, 128), BF),
-        pltpu.VMEM((8, WIDE), F32),
+        pltpu.VMEM((16, WIDE), F32),
+        pltpu.VMEM((16, WIDE), BF),
         pltpu.VMEM((2, TOK, SEQ), BF),
         pltpu.VMEM((TOK, 640), BF),
         pltpu.VMEM((8 * TOK, 512), BF),
@@ -380,21 +405,24 @@
         pltpu.VMEM((2, CTX, RC, 128), BF),
         pltpu.VMEM((2, TOK, 512), BF),
         pltpu.VMEM((2, TOK, 512), F32),
+        pltpu.VMEM((128, CH), F32),
         pltpu.VMEM((2, TOK, 512), BF),
         pltpu.VMEM((TOK, OUT), F32),
         *sums,
+        pltpu.VMEM((2, RC, OUT), BF),
         dma((9,)),
         dma((2,)),
         dma((2, 2)),
         dma((3, 2)),
-        dma((18,)),
-        dma((18,)),
+        dma((6 * NR,)),
+        dma((6 * NR,)),
+        dma((2 * NR,)),
     ]
     return pl.pallas_call(
         kernel,
         out_shape=jax.ShapeDtypeStruct((R, OUT), BF),
         in_specs=[hbm] * 8,
-        out_specs=vmem,
+        out_specs=hbm,
         scratch_shapes=scratch,
         compiler_params=pltpu.CompilerParams(
             collective_id=0, has_side_effects=True, vmem_limit_bytes=56 << 20

time: 66 us -> 66.1 us (level)
  no operation moved by 1% of the time
where the time goes in v2:
time: 66.1 us; the launch traced here: 65.7 us
  Pallas kernels  64 us (97%)
  local copies, waits for them, and re-layouts  1.67 us (3%)
    pallas_call x1, Pallas kernels, shards(): pl.pallas_call(kernel, out_shape=jax.ShapeDtypeStruct((R, OUT), BF), in_s...  64 us
    unnamed x1, local copies, waits for them, and re-layouts  1.67 us

profile of v2, /device:TPU:2, one launch (start us, length us, event | category | flops | bytes accessed | tf_op | source)
XLA Modules:
  0.0 65.7 jit_solution(6393180106807284463)
XLA Ops:
  0.0 64.0 %hyena.1 = bf16[32,4096]{1,0:T(8,128)(2,1)} custom-call(bf16[256,1024]{1,0:T(8,128)(2,1)} %k_hbm.1, bf16[256,1024]{1,0:T(8,128)(2,1)} %v_hbm.1, bf16[256,1024]{1,0:T(8,128)(2,1)} %q_hbm.1, f32[64,256]{1,0:T(8,128)} %bitcast.5, bf16[32,2,16,4096]{3,2,1,0:T(8,128)(2,1)} %bitcast.4, bf16[1024,1024]{1,0:T(8,128)(2,1)} %constant.2.clone.s_hbm, s32[1,64]{1,0:T(1,128)} %bitcast.7, ...), custom_call_target="tpu_custom_call" | custom-call | tf_op jit(solution)/shard_map/hyena/pallas_call | solution.py:421
  64.0 1.7 %copy.10 = bf16[32,4096]{1,0:T(8,128)(2,1)} copy(bf16[32,4096]{1,0:T(8,128)(2,1)} %hyena.1) | data formatting | bytes 524288

commit v3 on v2

--- a/solution.py
+++ b/solution.py
@@ -323,10 +323,9 @@
         mix(field0, 0, ck, R)
         chunk = slice(ck * 128, ck * 128 + 128)
 
-        @pl.loop(0, OUT // 512)
-        def _(n):
-            cols = pl.ds(pl.multiple_of(n * 512, 512), 512)
-            zacc[chunk, cols] = exact_dot(mixed[0, chunk, :], wbuf[0, :, :, cols].reshape(512, 512))
+        for n in range(0, OUT, 1024):
+            cols = slice(n, n + 1024)
+            zacc[chunk, cols] = exact_dot(mixed[0, chunk, :], wbuf[0, :, :, cols].reshape(512, 1024))
 
     for ck in range(2):
         project_first(ck)
@@ -339,16 +338,12 @@
         chunk = slice(ck * 128, ck * 128 + 128)
         for t, (first, width, ways) in enumerate(ROUTES):
             whole = sums[6 * t]
-
-            @pl.loop(0, width // 256)
-            def _(n):
-                at = pl.multiple_of(n * 256, 256)
-                cols = pl.ds(at + first, 256)
-                part = exact_dot(mixed[1, chunk, :], wbuf[1, :, :, cols].reshape(512, 256))
-                part = (part + zacc[chunk, cols]).astype(BF)
-                for p in range(8):
-                    to = [bit(p, way) for way in ways]
-                    whole[ck, to[0], to[1], to[2], :, pl.ds(at, 256)] = part[p * RC : p * RC + RC]
+            cols = slice(first, first + width)
+            part = exact_dot(mixed[1, chunk, :], wbuf[1, :, :, cols].reshape(512, width))
+            part = (part + zacc[chunk, cols]).astype(BF)
+            for p in range(8):
+                to = [bit(p, way) for way in ways]
+                whole[ck, to[0], to[1], to[2]] = part[p * RC : p * RC + RC]
 
             hop(ck, t, 0).start()
 

time: 66.1 us -> 63.6 us (0.962)
  Pallas kernels: 64 us -> 61.8 us
    pallas_call x1, Pallas kernels: 64 us -> 61.8 us  [shards(): pl.pallas_call(kernel, out_shape=jax.ShapeDtypeStruct((R, OUT), BF), in_s...]
where the time goes in v3:
time: 63.6 us; the launch traced here: 63.5 us
  Pallas kernels  61.8 us (97%)
  local copies, waits for them, and re-layouts  1.67 us (3%)
    pallas_call x1, Pallas kernels, shards(): pl.pallas_call(kernel, out_shape=jax.ShapeDtypeStruct((R, OUT), BF), in_s...  61.8 us
    unnamed x1, local copies, waits for them, and re-layouts  1.67 us

profile of v3, /device:TPU:2, one launch (start us, length us, event | category | flops | bytes accessed | tf_op | source)
XLA Modules:
  0.0 63.5 jit_solution(7456002800237803907)
XLA Ops:
  0.0 61.8 %hyena.1 = bf16[32,4096]{1,0:T(8,128)(2,1)} custom-call(bf16[256,1024]{1,0:T(8,128)(2,1)} %k_hbm.1, bf16[256,1024]{1,0:T(8,128)(2,1)} %v_hbm.1, bf16[256,1024]{1,0:T(8,128)(2,1)} %q_hbm.1, f32[64,256]{1,0:T(8,128)} %bitcast.5, bf16[32,2,16,4096]{3,2,1,0:T(8,128)(2,1)} %bitcast.4, bf16[1024,1024]{1,0:T(8,128)(2,1)} %constant.2.clone.s_hbm, s32[1,64]{1,0:T(1,128)} %bitcast.7, ...), custom_call_target="tpu_custom_call" | custom-call | tf_op jit(solution)/shard_map/hyena/pallas_call | solution.py:416
  61.8 1.7 %copy.10 = bf16[32,4096]{1,0:T(8,128)(2,1)} copy(bf16[32,4096]{1,0:T(8,128)(2,1)} %hyena.1) | data formatting | bytes 524288

commit v4 on v3

--- a/solution.py
+++ b/solution.py
@@ -31,10 +31,10 @@
 ROUTES = (
     (0, 768, ("x0", "x1", "z")),
     (768, 768, ("x1", "z", "x0")),
-    (1536, 768, ("z", "x0", "x1")),
-    (2304, 512, ("x0", "x1", "z")),
-    (2816, 768, ("x1", "z", "x0")),
-    (3584, 512, ("z", "x0", "x1")),
+    (1536, 640, ("z", "x0", "x1")),
+    (2176, 640, ("x0", "x1", "z")),
+    (2816, 640, ("x1", "z", "x0")),
+    (3456, 640, ("z", "x0", "x1")),
 )
 NR = len(ROUTES)
 
@@ -60,12 +60,12 @@
 
 
 def kernel(
-    k_hbm, v_hbm, q_hbm, f_hbm, w_hbm, s_hbm, l_hbm, d_hbm, out,
+    k_hbm, v_hbm, q_hbm, f_hbm, w_hbm, s_hbm, l_hbm, d_hbm, out, brought,
     kbuf, vbuf, qbuf, fbuf, wbuf, swap, lens, skip, gated, stage,
     fsend, frecv, xsend, xrecv, wide, turned, toep, xpad, xv, yacc, y0send, y0recv, y1send, y1recv, q_own, direct, field0, mixed, zacc,
     *rest,
 ):
-    sums, (obuf, load_sem, f_sem, x_sem, y_sem, rs_send, rs_recv, out_sem) = rest[:-8], rest[-8:]
+    sums, (load_sem, f_sem, x_sem, y_sem, rs_send, rs_recv, out_sem) = rest[:-7], rest[-7:]
     me = lax.axis_index("ctx")
     tp = lax.axis_index("tp")
     zl, x = tp // 4, lax.rem(tp, 4)
@@ -264,11 +264,15 @@
                 y1recv[ck, me] = y1send[ck, me]
                 send_all(y1send.at[ck], y1recv.at[ck], y_sem.at[1 + ck])
 
+    def piece(whole, ck, t):
+        first, width, _ = ROUTES[t]
+        return whole.at[pl.ds(ck * RC, RC), pl.ds(first, width)]
+
     def hop(ck, t, step):
-        whole, got0, kept1, got1, kept2, got2 = sums[6 * t : 6 * t + 6]
+        whole, got0, kept1, got1, kept2 = sums[5 * t : 5 * t + 5]
         way = ROUTES[t][2][step]
         source = (whole, kept1, kept2)[step].at[ck, 1 - mine[way]]
-        target = (got0, got1, got2)[step].at[ck]
+        target = (got0, got1)[step].at[ck] if step < 2 else piece(brought, ck, t)
         index = (ck * NR + t) * 3 + step
         return pltpu.make_async_remote_copy(
             source, target, rs_send.at[index], rs_recv.at[index],
@@ -276,17 +280,14 @@
         )
 
     def store(ck, t):
-        first, width, _ = ROUTES[t]
+        kept2 = sums[5 * t + 4]
         return pltpu.make_async_copy(
-            obuf.at[ck, :, pl.ds(first, width)],
-            out.at[pl.ds(ck * RC, RC), pl.ds(first, width)],
-            out_sem.at[ck * NR + t],
+            kept2.at[ck, mine[ROUTES[t][2][2]]], piece(out, ck, t), out_sem.at[ck * NR + t]
         )
 
     def add_up(ck, t, step):
-        whole, got0, kept1, got1, kept2, got2 = sums[6 * t : 6 * t + 6]
-        first, width, ways = ROUTES[t]
-        own = mine[ways[step]]
+        whole, got0, kept1, got1, kept2 = sums[5 * t : 5 * t + 5]
+        own = mine[ROUTES[t][2][step]]
         hop(ck, t, step).wait_recv()
         if step == 0:
             for i in range(2):
@@ -295,9 +296,6 @@
         elif step == 1:
             for i in range(2):
                 kept2[ck, i] = (kept1[ck, own, i].astype(F32) + got1[ck, i].astype(F32)).astype(BF)
-        else:
-            total = kept2[ck, own].astype(F32) + got2[ck].astype(F32)
-            obuf[ck, :, first : first + width] = total.astype(BF)
             store(ck, t).start()
 
     def mix(field, g, ck, count):
@@ -337,7 +335,7 @@
         mix(field, 1, ck, RC)
         chunk = slice(ck * 128, ck * 128 + 128)
         for t, (first, width, ways) in enumerate(ROUTES):
-            whole = sums[6 * t]
+            whole = sums[5 * t]
             cols = slice(first, first + width)
             part = exact_dot(mixed[1, chunk, :], wbuf[1, :, :, cols].reshape(512, width))
             part = (part + zacc[chunk, cols]).astype(BF)
@@ -371,7 +369,7 @@
     dma = pltpu.SemaphoreType.DMA
     sums = []
     for _, width, _ in ROUTES:
-        for lead in ((2, 2, 2), (2, 2), (2, 2), (2,), (2,), ()):
+        for lead in ((2, 2, 2), (2, 2), (2, 2), (2,), (2,)):
             sums.append(pltpu.VMEM((2,) + lead + (RC, width), BF))
     scratch = [
         pltpu.VMEM((TOK, CH), BF),
@@ -404,7 +402,6 @@
         pltpu.VMEM((2, TOK, 512), BF),
         pltpu.VMEM((TOK, OUT), F32),
         *sums,
-        pltpu.VMEM((2, RC, OUT), BF),
         dma((9,)),
         dma((2,)),
         dma((2, 2)),
@@ -413,11 +410,11 @@
         dma((6 * NR,)),
         dma((2 * NR,)),
     ]
-    return pl.pallas_call(
+    kept, brought = pl.pallas_call(
         kernel,
-        out_shape=jax.ShapeDtypeStruct((R, OUT), BF),
+        out_shape=[jax.ShapeDtypeStruct((R, OUT), BF)] * 2,
         in_specs=[hbm] * 8,
-        out_specs=hbm,
+        out_specs=[hbm] * 2,
         scratch_shapes=scratch,
         compiler_params=pltpu.CompilerParams(
             collective_id=0, has_side_effects=True, vmem_limit_bytes=56 << 20
@@ -427,6 +424,7 @@
         k_proj, v_proj, q_proj, filters.T, out_weight.reshape(CTX, 2, C16, OUT), swap,
         lengths.reshape(1, GRP), skip_gain.reshape(1, CH),
     )
+    return (kept.astype(F32) + brought.astype(F32)).astype(BF)
 
 
 def solution(mesh):

time: 63.6 us -> 62.9 us (0.989)
  other arithmetic: 0 us -> 1.79 us
  local copies, waits for them, and re-layouts: 1.67 us -> 0 us
  Pallas kernels: 61.8 us -> 61 us
    convert_element_type x0 -> x1, other arithmetic: none -> 1.79 us  [shards(): return (kept.astype(F32) + brought.astype(F32)).astype(BF)]
    unnamed x1 -> x0, local copies, waits for them, and re-layouts: 1.67 us -> none
    pallas_call x1, Pallas kernels: 61.8 us -> 61 us  [shards(): pl.pallas_call(kernel, out_shape=[jax.ShapeDtypeStruct((R, OUT), BF)] * 2...]
where the time goes in v4:
time: 62.9 us; the launch traced here: 62.8 us
  Pallas kernels  61 us (97%)
  other arithmetic  1.79 us (3%)
    pallas_call x1, Pallas kernels, shards(): pl.pallas_call(kernel, out_shape=[jax.ShapeDtypeStruct((R, OUT), BF)] * 2...  61 us
    convert_element_type x1, other arithmetic, shards(): return (kept.astype(F32) + brought.astype(F32)).astype(BF)  1.79 us

profile of v4, /device:TPU:2, one launch (start us, length us, event | category | flops | bytes accessed | tf_op | source)
XLA Modules:
  0.0 62.8 jit_solution(15299801745980549197)
XLA Ops:
  0.0 61.0 %hyena.1 = (bf16[32,4096]{1,0:T(8,128)(2,1)}, bf16[32,4096]{1,0:T(8,128)(2,1)}) custom-call(bf16[256,1024]{1,0:T(8,128)(2,1)} %k_hbm.1, bf16[256,1024]{1,0:T(8,128)(2,1)} %v_hbm.1, bf16[256,1024]{1,0:T(8,128)(2,1)} %q_hbm.1, f32[64,256]{1,0:T(8,128)} %bitcast.5, bf16[32,2,16,4096]{3,2,1,0:T(8,128)(2,1)} %bitcast.4, bf16[1024,1024]{1,0:T(8,128)(2,1)} %constant.2.clone.s_hbm, ...), custom_call_target="tpu_custom_call" | custom-call | tf_op jit(solution)/shard_map/hyena/pallas_call | solution.py:413
  61.0 1.8 %add_convert_fusion = bf16[32,4096]{1,0:T(8,128)(2,1)} fusion(bf16[32,4096]{1,0:T(8,128)(2,1)} %get-tuple-element.8, bf16[32,4096]{1,0:T(8,128)(2,1)} %get-tuple-element.7), kind=kLoop, calls=%fused_computation | loop fusion | flops 524288 | bytes 786432 | tf_op jit(solution)/shard_map/convert_element_type | solution.py:427

commit v5 on v4

--- a/solution.py
+++ b/solution.py
@@ -165,7 +165,8 @@
     q_load = load(q_hbm, qbuf, 6)
     w_loads = [load(w_hbm.at[:, g], wbuf.at[g], 7 + g) for g in range(2)]
     waiter(fsend, frecv, f_sem).wait_recv()
-    for g in range(2):
+
+    def build(g):
         for n in range(2 * CTX):
             tap_row = frecv[CTX - 1 - n // 2, g * 2 + n % 2 : g * 2 + n % 2 + 1, :]
             wide[:, n * 128 : n * 128 + 128] = jnp.broadcast_to(tap_row, (16, 128))
@@ -209,6 +210,7 @@
 
     xpad[:, :128] = jnp.zeros((TOK, 128), BF)
     for g in range(2):
+        build(g)
         waiter(xsend.at[g], xrecv.at[g], x_sem.at[g]).wait_recv()
         for b in range(CTX):
             stage[(b // 8) * R : (b // 8) * R + R, (b % 8) * 128 : (b % 8) * 128 + 128] = xrecv[g, b]
@@ -251,7 +253,6 @@
                     y0send[b, ck * RC : ck * RC + RC] = packed[at : at + RC, lane : lane + 128]
             y0recv[me] = y0send[me]
             send_all(y0send, y0recv, y_sem.at[0])
-            split_groups()
         else:
             for ck in range(2):
                 convolve(slice(ck * 128, ck * 128 + 128))
@@ -309,6 +310,7 @@
                     q_own[g, rows, lane].astype(F32) * (conv + direct[g, rows, lane])
                 ).astype(BF)
 
+    split_groups()
     waiter(y0send, y0recv, y_sem.at[0]).wait_recv()
     for e in range(CTX):
         o, i = e // 8, e % 8
@@ -325,8 +327,10 @@
             cols = slice(n, n + 1024)
             zacc[chunk, cols] = exact_dot(mixed[0, chunk, :], wbuf[0, :, :, cols].reshape(512, 1024))
 
+    project_first(0)
+    project_first(1)
+
     for ck in range(2):
-        project_first(ck)
         waiter(y1send.at[ck], y1recv.at[ck], y_sem.at[1 + ck]).wait_recv()
         for e in range(CTX):
             o, i = e // 8, e % 8

time: 62.9 us -> 62.2 us (0.989)
  Pallas kernels: 61 us -> 60.3 us
    pallas_call x1, Pallas kernels: 61 us -> 60.3 us  [shards(): pl.pallas_call(kernel, out_shape=[jax.ShapeDtypeStruct((R, OUT), BF)] * 2...]
where the time goes in v5:
time: 62.2 us; the launch traced here: 62.1 us
  Pallas kernels  60.3 us (97%)
  other arithmetic  1.79 us (3%)
    pallas_call x1, Pallas kernels, shards(): pl.pallas_call(kernel, out_shape=[jax.ShapeDtypeStruct((R, OUT), BF)] * 2...  60.3 us
    convert_element_type x1, other arithmetic, shards(): return (kept.astype(F32) + brought.astype(F32)).astype(BF)  1.79 us

profile of v5, /device:TPU:2, one launch (start us, length us, event | category | flops | bytes accessed | tf_op | source)
XLA Modules:
  0.0 62.1 jit_solution(8380358838691500977)
XLA Ops:
  0.0 60.3 %hyena.1 = (bf16[32,4096]{1,0:T(8,128)(2,1)}, bf16[32,4096]{1,0:T(8,128)(2,1)}) custom-call(bf16[256,1024]{1,0:T(8,128)(2,1)} %k_hbm.1, bf16[256,1024]{1,0:T(8,128)(2,1)} %v_hbm.1, bf16[256,1024]{1,0:T(8,128)(2,1)} %q_hbm.1, f32[64,256]{1,0:T(8,128)} %bitcast.5, bf16[32,2,16,4096]{3,2,1,0:T(8,128)(2,1)} %bitcast.4, bf16[1024,1024]{1,0:T(8,128)(2,1)} %constant.2.clone.s_hbm, ...), custom_call_target="tpu_custom_call" | custom-call | tf_op jit(solution)/shard_map/hyena/pallas_call | solution.py:417
  60.3 1.8 %add_convert_fusion = bf16[32,4096]{1,0:T(8,128)(2,1)} fusion(bf16[32,4096]{1,0:T(8,128)(2,1)} %get-tuple-element.8, bf16[32,4096]{1,0:T(8,128)(2,1)} %get-tuple-element.7), kind=kLoop, calls=%fused_computation | loop fusion | flops 524288 | bytes 786432 | tf_op jit(solution)/shard_map/convert_element_type | solution.py:431
